TPU v7x, 128 devices: a whole 4x4x4 slice. The times are simulated.
128 devices in a mesh: dp: 32 (over z, y, core), mp: 4 (over x).
Axes of the slice: x: 4, y: 4, z: 4, core: 2. Of those that a mesh axis runs over, the one named last changes fastest.
Arguments:
- patches: bfloat16 [49152, 128], P(('dp', 'mp')), may hold values from -6 to 6
- row_count: int32 [128], P(('dp', 'mp')), may hold values from 0 to 384, as said below
- target_group: int32 [49152], P(('dp', 'mp')), may hold values from 0 to 31, as said below
- target_offset: int32 [49152], P(('dp', 'mp')), may hold values from 0 to 639, as said below
- embed: bfloat16 [128, 6144], replicated, may hold values from -0.5 to 0.5
- norm_gain: bfloat16 [6144], replicated, may hold values from 0.099609375 to 1.8984375
- readout: bfloat16 [6144, 128], P('mp'), may hold values from -0.078125 to 0.078125
- target: bfloat16 [20480, 128], P('dp'), may hold values from -12 to 12
- master: float32 [6144, 6144], P('dp', 'mp'), may hold values from -6 to 6
- moment1: float32 [6144, 6144], P('dp', 'mp'), may hold values from -2 to 2
- moment2: float32 [6144, 6144], P('dp', 'mp'), may hold values from 0.0034722222 to 0.1388889
Outputs:
- prediction: float32 [20480, 128], P('dp')
- master_new: float32 [6144, 6144], P('dp', 'mp')
- moment1_new: float32 [6144, 6144], P('dp', 'mp')
- moment2_new: float32 [6144, 6144], P('dp', 'mp')
- weight_copy: bfloat16 [6144, 6144], P('dp', 'mp')
Inputs may be any that keep to these rules, and one draw needn't show every extreme that they name: Device i holds its live patch rows in its first row_count[i] slots; some device holds 384 of them in every draw. Over the live slots of all devices, each pair (target_group, target_offset) of the 20480 positions occurs exactly once; values in slots past row_count are arbitrary within the range. Call target_offset // 160 the block of a row. Each (batch, block) receives exactly 160 live rows; one device sends at most 3 live rows to one (batch, block), and every (batch, block) gets 3 rows from some device.
All inputs are finite; a program needn't handle non-finite values.
Results may differ from a plain program's by a relative error of at most 0.03.
Values may be sent and summed in bfloat16 or wider, within the bound.
A program may use at most 128 MiB of HBM per device.

v0:
```python
import jax
import jax.numpy as jnp
from jax import lax
from jax.sharding import PartitionSpec as P

gelu_const = 0.7978845608028654
beta_one = 0.9
beta_two = 0.95
learn_rate = 0.01
decay_rate = 0.1
adam_epsilon = 1e-08
step_count = 20


def gelu_tanh(value):
    inner = gelu_const * (value + 0.044715 * value * value * value)
    return 0.5 * value * (1.0 + jnp.tanh(inner))


def gelu_slope(value):
    tangent = jnp.tanh(gelu_const * (value + 0.044715 * value * value * value))
    return 0.5 * (1.0 + tangent) + 0.5 * value * (1.0 - tangent * tangent) * gelu_const * (
        1.0 + 3.0 * 0.044715 * value * value
    )


def shards(
    patches,
    row_count,
    target_group,
    target_offset,
    embed,
    norm_gain,
    readout,
    target,
    master,
    moment1,
    moment2,
):
    model_count = lax.axis_size("mp")
    batch_count = lax.axis_size("dp")
    devices_all = batch_count * model_count
    slot_total = patches.shape[0]
    capacity = slot_total // devices_all
    batch_rows = target.shape[0]
    block_rows = batch_rows // model_count
    width = embed.shape[1]
    patch_width = patches.shape[1]
    occupied = jnp.arange(slot_total, dtype=jnp.int32) < row_count[0]
    owner_index = jnp.where(
        occupied, target_group * model_count + target_offset // block_rows, devices_all
    )
    onehot = (owner_index[:, None] == jnp.arange(devices_all, dtype=jnp.int32)[None, :]).astype(
        jnp.int32
    )
    running = jnp.cumsum(onehot, axis=0)
    placing = jnp.sum(onehot * running, axis=1) - 1
    send_slot = jnp.where(occupied, owner_index * capacity + placing, devices_all * capacity)
    outgoing = (
        jnp.zeros((devices_all * capacity, patch_width), jnp.bfloat16)
        .at[send_slot]
        .set(patches, mode="drop")
    )
    slot_marks = (
        jnp.full((devices_all * capacity,), block_rows, jnp.int32)
        .at[send_slot]
        .set(target_offset % block_rows, mode="drop")
    )
    arrived, arrived_marks = (
        lax.all_to_all(outgoing, ("dp", "mp"), split_axis=0, concat_axis=0, tiled=True),
        lax.all_to_all(slot_marks, ("dp", "mp"), split_axis=0, concat_axis=0, tiled=True),
    )
    block_patches = (
        jnp.zeros((block_rows, patch_width), jnp.bfloat16)
        .at[arrived_marks]
        .set(arrived, mode="drop")
    )
    gain_wide = norm_gain.astype(jnp.float32)
    hidden = gelu_tanh(
        jnp.dot(
            lax.all_gather(block_patches, "mp", axis=0, tiled=True),
            embed,
            preferred_element_type=jnp.float32,
        )
    )
    normed = (
        hidden * lax.rsqrt(jnp.mean(hidden * hidden, axis=-1, keepdims=True) + 1e-05) * gain_wide
    ).astype(jnp.bfloat16)
    weight = master.astype(jnp.bfloat16)
    width_scale = 1.0 / width**0.5
    columns = normed
    preact = (
        jnp.dot(
            columns,
            lax.all_gather(weight, "dp", axis=0, tiled=True),
            preferred_element_type=jnp.float32,
        )
        * width_scale
    )
    activation = gelu_tanh(preact).astype(jnp.bfloat16)
    prediction = lax.psum(
        jnp.dot(activation, readout, preferred_element_type=jnp.float32).astype(jnp.bfloat16), "mp"
    ).astype(jnp.float32)
    errors = (prediction - target.astype(jnp.float32)).astype(jnp.bfloat16)
    backward = lax.dot_general(
        errors, readout, (((1,), (1,)), ((), ())), preferred_element_type=jnp.float32
    )
    delta_rows = (backward * gelu_slope(preact)).astype(jnp.bfloat16)
    columns = normed
    gradient = lax.psum_scatter(
        (
            lax.dot_general(
                columns, delta_rows, (((0,), (0,)), ((), ())), preferred_element_type=jnp.float32
            )
            * width_scale
        ).astype(jnp.bfloat16),
        "dp",
        scatter_dimension=0,
        tiled=True,
    ).astype(jnp.float32)
    moment1_new = beta_one * moment1 + (1.0 - beta_one) * gradient
    moment2_new = beta_two * moment2 + (1.0 - beta_two) * gradient * gradient
    first_fix = moment1_new / (1.0 - beta_one**step_count)
    second_fix = moment2_new / (1.0 - beta_two**step_count)
    master_new = master - learn_rate * (
        first_fix / (jnp.sqrt(second_fix) + adam_epsilon) + decay_rate * master
    )
    return (prediction, master_new, moment1_new, moment2_new, master_new.astype(jnp.bfloat16))


def solution(mesh):
    placed = (
        P(("dp", "mp"), None),
        P(("dp", "mp")),
        P(("dp", "mp")),
        P(("dp", "mp")),
        P(),
        P(),
        P("mp", None),
        P("dp", None),
        P("dp", "mp"),
        P("dp", "mp"),
        P("dp", "mp"),
    )
    return jax.shard_map(
        shards,
        mesh=mesh,
        in_specs=placed,
        out_specs=(P("dp", None), P("dp", "mp"), P("dp", "mp"), P("dp", "mp"), P("dp", "mp")),
        check_vma=False,
    )
```

profile of v0, /device:TPU:0, one launch (start us, length us, event | category | flops | bytes accessed | tf_op | source)
XLA Modules:
  0.0 316.7 jit_solution(15524870666545750787)
XLA Ops:
  7.2 0.0 copy-start
  7.2 0.0 copy-start.4
  7.2 0.0 all-gather.2.cloned.1.call-start
  7.2 2.3 convert_element_type.44
  9.5 0.0 all-gather.2.cloned.1.call-update
  10.2 0.7 add_select_fusion
  10.9 0.1 copy.18
  11.0 0.2 fusion.14
  11.3 0.1 broadcast_add_fusion
  11.3 0.2 fusion.16
  11.6 2.9 scatter_custom_fusion
  14.5 0.8 all_to_all.16
  15.3 11.1 %all-to-all-start = ((s32[128,3,1]{1,2,0:T(1,128)}), s32[128,3,1]{1,2,0:T(1,128)S(1)}, u32[]{:S(2)}, u32[]{:S(2)}) async-start(s32[128,3,1]{1,2,0:T(1,128)} %bitcast.5), calls=%async_computation | async-start | bytes 131072 | tf_op jit(solution)/shard_map/all_to_all | solution.py:71
  26.5 0.0 copy-done.4
  26.5 1.8 scatter_custom_fusion.1
  28.3 0.7 all_to_all.19
  29.0 6.7 %all-to-all-done = s32[128,3,1]{1,2,0:T(1,128)S(1)} async-done(((s32[128,3,1]{1,2,0:T(1,128)}), s32[128,3,1]{1,2,0:T(1,128)S(1)}, u32[]{:S(2)}, u32[]{:S(2)}) %all-to-all-start) | async-done | bytes 1568 | tf_op jit(solution)/shard_map/all_to_all | solution.py:71
  35.7 4.6 %all-to-all-start.1 = ((bf16[128,3,128]{2,1,0:T(4,128)(2,1)}), bf16[128,3,128]{2,1,0:T(4,128)(2,1)S(1)}, u32[]{:S(2)}, u32[]{:S(2)}) async-start(bf16[128,3,128]{2,1,0:T(4,128)(2,1)} %all_to_all.19), calls=%async_computation.1 | async-start | bytes 262144 | tf_op jit(solution)/shard_map/all_to_all | solution.py:70
  40.4 0.0 all-reduce.2.cloned.1.call-start
  40.4 0.5 broadcast.113
  40.9 0.8 reduce.5
  41.7 0.2 all_to_all.18
  42.0 7.9 %all-to-all-done.1 = bf16[128,3,128]{2,1,0:T(4,128)(2,1)S(1)} async-done(((bf16[128,3,128]{2,1,0:T(4,128)(2,1)}), bf16[128,3,128]{2,1,0:T(4,128)(2,1)S(1)}, u32[]{:S(2)}, u32[]{:S(2)}) %all-to-all-start.1) | async-done | bytes 98336 | tf_op jit(solution)/shard_map/all_to_all | solution.py:70
  49.8 0.1 reshape.88
  49.9 1.4 scatter_custom_fusion.2
  51.4 12.2 %all_gather.6 = bf16[640,128]{1,0:T(8,128)(2,1)S(1)} all-gather(bf16[160,128]{1,0:T(8,128)(2,1)S(1)} %scatter_custom_fusion.2), channel_id=1, replica_groups=mesh['dp'=32,'mp'=4] {'mp'}, dimensions={0}, use_global_device_ids=true | all-gather | bytes 204800 | tf_op jit(solution)/shard_map/all_gather | solution.py:81
  63.6 0.0 copy-done
  63.6 9.0 %multiply_reduce_fusion = (f32[640]{0:T(1024)S(1)}, f32[640,6144]{1,0:T(8,128)}) fusion(bf16[640,128]{1,0:T(8,128)(2,1)S(1)} %all_gather.6, bf16[128,6144]{1,0:T(8,128)(2,1)S(1)} %copy-done), kind=kOutput, calls=%fused_computation.10 | convolution fusion | flops 1045953920 | bytes 17467904 | tf_op jit(solution)/shard_map/dot_general | solution.py:80
  72.6 19.0 %all-gather.2.cloned.1.call-done = bf16[6144,1536]{1,0:T(8,128)(2,1)} async-done(((bf16[192,1536]{1,0:T(8,128)(2,1)}), bf16[6144,1536]{1,0:T(8,128)(2,1)}) %all-gather.2.cloned.1.call-update) | async-done | bytes 18874384 | tf_op jit(solution)/shard_map/all_gather | solution.py:95
  91.6 18.6 %fusion.40 = f32[640,1536]{1,0:T(8,128)S(1)} fusion(bf16[6144,1536]{1,0:T(8,128)(2,1)} %all-gather.2.cloned.1.call-done, f32[640,6144]{1,0:T(8,128)} %get-tuple-element.12, f32[6144]{0:T(1024)S(1)} %convert_element_type.42, f32[640]{0:T(1024)S(1)} %add_rsqrt_fusion), kind=kOutput, calls=%fused_computation.67 | convolution fusion | flops 12091392000 | bytes 38562304 | tf_op jit(solution)/shard_map/dot_general | solution.py:93
  110.2 0.0 copy-start.7
  110.2 2.0 copy-done.7
  112.2 0.0 copy-done.5
  112.2 2.2 fusion.13
  114.4 0.0 all-reduce.2.cloned.1.call-update
  114.4 0.3 reduce-scatter.2.cloned.1.call-start
  114.7 40.5 %all-reduce.2.cloned.1.call-done = bf16[640,128]{1,0:T(8,128)(2,1)} async-done(((bf16[640,128]{1,0:T(8,128)(2,1)}), bf16[640,128]{1,0:T(8,128)(2,1)}) %all-reduce.2.cloned.1.call-update) | async-done | bytes 163856 | tf_op jit(solution)/shard_map/psum | solution.py:101
  155.2 0.9 convert_element_type.47
  156.1 0.0 copy-done.6
  156.1 0.0 copy-start.3
  156.1 27.2 %multiply_convert_fusion = bf16[6144,1536]{1,0:T(8,128)(2,1)} fusion(f32[640,1536]{1,0:T(8,128)} %copy-done.7, bf16[1536,128]{1,0:T(8,128)(2,1)S(1)} %copy-done.5, f32[640,128]{1,0:T(8,128)S(1)} %convert_element_type.47, bf16[640,128]{1,0:T(8,128)(2,1)S(1)} %copy-done.6, f32[640,6144]{1,0:T(8,128)} %get-tuple-element.12, f32[6144]{0:T(1024)S(1)} %convert_element_type.42, ...), kind=kOutput, calls=%fused_computation.3 | convolution fusion | flops 12381831168 | bytes 39447040 | tf_op jit(solution)/shard_map/dot_general | solution.py:112
  183.4 0.0 copy-done.3
  183.4 0.0 reduce-scatter.2.cloned.1.call-update
  183.4 0.0 copy-start.1
  183.4 122.3 %reduce-scatter.2.cloned.1.call-done = bf16[192,1536]{1,0:T(8,128)(2,1)} async-done(((bf16[6144,1536]{1,0:T(8,128)(2,1)}), bf16[192,1536]{1,0:T(8,128)(2,1)}) %reduce-scatter.2.cloned.1.call-update) | async-done | bytes 589840 | tf_op jit(solution)/shard_map/reduce_scatter | solution.py:110
  305.7 0.0 copy-done.2
  305.7 4.4 %fusion.41 = (bf16[192,1536]{1,0:T(8,128)(2,1)}, f32[192,1536]{1,0:T(8,128)}, f32[192,1536]{1,0:T(8,128)}, f32[192,1536]{1,0:T(8,128)}) fusion(f32[192,1536]{1,0:T(8,128)S(1)} %copy-done.2, bf16[192,1536]{1,0:T(8,128)(2,1)} %reduce-scatter.2.cloned.1.call-done, f32[192,1536]{1,0:T(8,128)} %param.20, f32[192,1536]{1,0:T(8,128)} %param.21), kind=kLoop, calls=%fused_computation.68 | loop fusion | flops 5013504 | bytes 8257536 | tf_op jit(solution)/shard_map/convert_element_type | solution.py:128
  310.1 0.0 copy-done.1
  (10 shorter events, 0.1 us)
Async XLA Ops:
  7.2 56.4 %copy-start = (bf16[128,6144]{1,0:T(8,128)(2,1)S(1)}, bf16[128,6144]{1,0:T(8,128)(2,1)}, u32[]{:S(2)}) copy-start(bf16[128,6144]{1,0:T(8,128)(2,1)} %param.15) | copy-start | bytes 4718596
  7.2 19.3 %copy-start.4 = (bf16[6144]{0:T(1024)(128)(2,1)S(1)}, bf16[6144]{0:T(1024)(128)(2,1)}, u32[]{:S(2)}) copy-start(bf16[6144]{0:T(1024)(128)(2,1)} %param.16) | copy-start | bytes 36868
  7.2 84.4 %all-gather.2.cloned.1.call-start = ((), (), s32[]{:S(2)}) async-start(), calls=%async_computation.3 | async-start | bytes 19464192 | tf_op jit(solution)/shard_map/all_gather | solution.py:95
  15.3 20.4 %all-to-all-start = ((s32[128,3,1]{1,2,0:T(1,128)}), s32[128,3,1]{1,2,0:T(1,128)S(1)}, u32[]{:S(2)}, u32[]{:S(2)}) async-start(s32[128,3,1]{1,2,0:T(1,128)} %bitcast.5), calls=%async_computation | async-start | bytes 131072 | tf_op jit(solution)/shard_map/all_to_all | solution.py:71
  35.7 14.1 %all-to-all-start.1 = ((bf16[128,3,128]{2,1,0:T(4,128)(2,1)}), bf16[128,3,128]{2,1,0:T(4,128)(2,1)S(1)}, u32[]{:S(2)}, u32[]{:S(2)}) async-start(bf16[128,3,128]{2,1,0:T(4,128)(2,1)} %all_to_all.19), calls=%async_computation.1 | async-start | bytes 262144 | tf_op jit(solution)/shard_map/all_to_all | solution.py:70
  40.4 114.8 %all-reduce.2.cloned.1.call-start = ((), (), s32[]{:S(2)}) async-start(), calls=%async_computation.4 | async-start | bytes 327680 | tf_op jit(solution)/shard_map/psum | solution.py:101
  91.6 20.6 %copy-start.5 = (bf16[1536,128]{1,0:T(8,128)(2,1)S(1)}, bf16[1536,128]{1,0:T(8,128)(2,1)}, u32[]{:S(2)}) copy-start(bf16[1536,128]{1,0:T(8,128)(2,1)} %param.17) | copy-start | bytes 1179652
  110.2 2.0 copy-start.7
  112.2 43.9 %copy-start.6 = (bf16[640,128]{1,0:T(8,128)(2,1)S(1)}, bf16[640,128]{1,0:T(8,128)(2,1)}, u32[]{:S(2)}) copy-start(bf16[640,128]{1,0:T(8,128)(2,1)} %param.18) | copy-start | bytes 491524
  114.4 191.3 %reduce-scatter.2.cloned.1.call-start = ((), (), s32[]{:S(2)}) async-start(), calls=%async_computation.5 | async-start | bytes 19464192 | tf_op jit(solution)/shard_map/reduce_scatter | solution.py:110
  156.1 27.3 %copy-start.3 = (f32[640,128]{1,0:T(8,128)}, f32[640,128]{1,0:T(8,128)S(1)}, u32[]{:S(2)}) copy-start(f32[640,128]{1,0:T(8,128)S(1)} %convert_element_type.47) | copy-start | bytes 983044
  183.4 122.3 %copy-start.2 = (f32[192,1536]{1,0:T(8,128)S(1)}, f32[192,1536]{1,0:T(8,128)}, u32[]{:S(2)}) copy-start(f32[192,1536]{1,0:T(8,128)} %param.19) | copy-start | bytes 3538948
  183.4 126.7 %copy-start.1 = (bf16[128,6144]{1,0:T(8,128)(2,1)S(1)}, bf16[128,6144]{1,0:T(8,128)(2,1)}, u32[]{:S(2)}) copy-start(bf16[128,6144]{1,0:T(8,128)(2,1)} %param.15) | copy-start | bytes 4718596
Sparse Core Ops, SparseCore 0:
  10.9 80.6 all-gather.1
  114.5 40.6 all-reduce.1
  183.5 122.1 reduce-scatter.1
where the time goes:
time: 317 us
  waiting for transfers between devices  196 us (62%)
  matrix products  57 us (18%)
  starting transfers between devices  16.1 us (5%)
  between operations  14.6 us (5%)
  blocking collectives  12.2 us (4%)
  local copies, waits for them, and re-layouts  10.7 us (3%)
  other arithmetic  9.67 us (3%)
    reduce_scatter x1, waiting for transfers between devices, shards(): lax.psum_scatter((lax.dot_general(columns, delta_rows, (((0,), (0,)), (()...  122 us
    psum x1, waiting for transfers between devices, shards(): lax.psum(jnp.dot(activation, readout, preferred_element_type=jnp.float32)...  40.5 us
    dot_general x1, matrix products, shards(): lax.dot_general(columns, delta_rows, (((0,), (0,)), ((), ())), preferred_...  27.2 us
    all_gather x1, waiting for transfers between devices, shards(): lax.all_gather(weight, 'dp', axis=0, tiled=True)  19 us
    dot_general x1, matrix products, shards(): jnp.dot(columns, lax.all_gather(weight, 'dp', axis=0, tiled=True), prefer...  18.6 us
    all_gather x1, blocking collectives, shards(): lax.all_gather(block_patches, 'mp', axis=0, tiled=True)  12.2 us
    all_to_all x1, starting transfers between devices, shards(): lax.all_to_all(slot_marks, ('dp', 'mp'), split_axis=0, concat_axis=0, til...  11.1 us
    dot_general x1, matrix products, shards(): jnp.dot(lax.all_gather(block_patches, 'mp', axis=0, tiled=True), embed, p...  8.99 us
  transfers between devices with their start and end apart: 5, of which 5 were waited for; matrix products, arithmetic and copies ran while one was open for 6% of the time, Pallas kernels for 0%

commit v1 on v0

v1 whole, which is shorter than its diff:
```python
import jax
import jax.numpy as jnp
from jax import lax
from jax.experimental import pallas as pl
from jax.experimental.pallas import tpu as pltpu
from jax.sharding import PartitionSpec as P

gelu_const = 0.7978845608028654
cubic = 0.044715
beta_one = 0.9
beta_two = 0.95
learn_rate = 0.01
decay_rate = 0.1
adam_epsilon = 1e-08
step_count = 20

WIDTH = 6144
ROWS = 192
COLS = 768
TOKENS = 1280
BLOCK = 160
SLOTS = 384
SCALE = 1.0 / WIDTH**0.5
MESH = pl.DeviceIdType.MESH
f32, bf16, i32 = jnp.float32, jnp.bfloat16, jnp.int32

NN = (((1,), (0,)), ((), ()))
NT = (((1,), (1,)), ((), ()))
TN = (((0,), (0,)), ((), ()))


def matmul(a, b, dims=NN):
    return lax.dot_general(a, b, dims, preferred_element_type=f32)


def iota(shape, axis):
    return lax.broadcasted_iota(i32, shape, axis)


def kernel(
    row_count,
    patches,
    group_row,
    offset_row,
    gain,
    embed_hbm,
    readout_hbm,
    target_hbm,
    master_hbm,
    pred_out,
    grad_out,
    emb,
    ro,
    tgt,
    master_own,
    master_far,
    far_half,
    w,
    hg,
    acc,
    delta,
    ssq,
    perm,
    out1,
    in1,
    out2,
    in2,
    batch,
    part_out,
    part_in,
    part_own,
    err_own,
    err_in,
    core_in,
    zhalf_in,
    zfull_in,
    y_in,
    pair_in,
    local_sem,
    r1_send,
    r1_recv,
    r2_send,
    r2_recv,
    r3_send,
    r3_recv,
    ag_send,
    ag_recv,
    part_send,
    part_recv,
    err_send,
    err_recv,
    rs_send,
    rs_recv,
):
    dp, x = lax.axis_index("dp"), lax.axis_index("mp")
    z = lax.div(dp, 8)
    y = lax.rem(lax.div(dp, 2), 4)
    c = lax.rem(dp, 2)
    k = lax.div(y, 2)
    p = lax.rem(y, 2)
    half = lax.rem(p + k, 2)
    yp = y + 1 - 2 * p
    ya = 3 - y
    yap = 3 - yp
    kk, oc = 1 - k, 1 - c
    zp, zm, z2 = lax.rem(z + 1, 4), lax.rem(z + 3, 4), lax.rem(z + 2, 4)
    member = z * 4 + k * 2 + c
    sub = p * 4 + x
    zs = (z, zp, zm, z2)
    ys = (y, yp, ya, yap)

    def device(zz, yy, cc, xx):
        return ((zz * 4 + yy) * 2 + cc, xx)

    def member_device(i):
        other = lax.rem(member + i, 16)
        zz, kz, cc = lax.div(other, 4), lax.rem(lax.div(other, 2), 2), lax.rem(other, 2)
        return other, device(zz, 2 * kz + p, cc, x)

    def sub_device(i):
        other = lax.rem(sub + i, 8)
        return other, device(z, 2 * k + lax.div(other, 4), c, lax.rem(other, 4))

    def remote(src, dst, send, recv, to):
        return pltpu.make_async_remote_copy(
            src_ref=src, dst_ref=dst, send_sem=send, recv_sem=recv, device_id=to, device_id_type=MESH
        )

    def chunk(zz, yy, cc, low=0, count=ROWS):
        start = pl.multiple_of(lax.rem(yy, 2) * (2 * ROWS) + cc * ROWS + low, 32)
        return w.at[zz * 2 + lax.div(yy, 2), pl.ds(start, count), :]

    def span(index, size, count=None):
        return pl.ds(pl.multiple_of(index * size, size), size if count is None else count)

    barrier = pltpu.get_barrier_semaphore()
    peers = [member_device(i)[1] for i in range(1, 16)]
    peers += [sub_device(i)[1] for i in range(1, 8)]
    peers += [device(z, ya, c, x)]
    for peer in peers:
        pl.semaphore_signal(barrier, inc=1, device_id=peer, device_id_type=MESH)

    loads = [
        (master_hbm.at[:, span(half, COLS)], master_own),
        (master_hbm.at[:, span(1 - half, COLS)], master_far),
        (embed_hbm, emb),
        (readout_hbm.at[span(half, COLS), :], ro),
        (target_hbm, tgt),
    ]
    loads = [pltpu.make_async_copy(a, b, local_sem.at[i]) for i, (a, b) in enumerate(loads)]
    for load in loads:
        load.start()

    group, offset = group_row[...], offset_row[...]
    live = iota((1, SLOTS), 1) < row_count[0]
    to_member = (group >> 3) * 4 + ((group >> 2) & 1) * 2 + (group & 1)
    block = sum((offset >= BLOCK * i).astype(i32) for i in range(1, 4))
    place = offset - block * BLOCK + 1
    to_sub = ((group >> 1) & 1) * 4 + block
    key = jnp.where(live, to_member * 8 + to_sub, -1)
    row_id, col_id = iota((SLOTS, SLOTS), 0), iota((SLOTS, SLOTS), 1)

    def column(values):
        wide = jnp.broadcast_to(values.astype(f32), (SLOTS, SLOTS))
        return jnp.sum(jnp.where(row_id == col_id, wide, 0.0), axis=1, keepdims=True)

    same = (column(key) == key.astype(f32)) & (row_id < col_id)
    rank = jnp.sum(jnp.where(same, 1.0, 0.0), axis=0, keepdims=True).astype(i32)
    slot = jnp.where(live, to_member * 32 + rank * 8 + to_sub, -1)
    pick = jnp.where(iota((512, SLOTS), 0) == slot, 1.0, 0.0).astype(bf16)
    marks = jnp.broadcast_to(column(place), (SLOTS, 128)).astype(bf16)
    out1[:, :128] = matmul(pick, patches[...]).astype(bf16)
    out1[:, 128:] = matmul(pick, marks).astype(bf16)

    loads[0].wait()
    loads[1].wait()
    own = chunk(z, y, c)
    own[...] = master_own[...].astype(bf16)
    far_half[...] = master_far[...].astype(bf16)

    pl.semaphore_wait(barrier, len(peers))

    sends = []

    def launch(copy):
        copy.start()
        sends.append(copy)

    for i in range(1, 16):
        other, to = member_device(i)
        launch(
            remote(
                out1.at[span(other, 32), :],
                in1.at[span(member, 32), :],
                r1_send.at[other],
                r1_recv.at[member],
                to,
            )
        )

    gathers = []

    def gather(event, src, dst, to):
        copy = remote(src, dst, ag_send.at[event], ag_recv.at[event], to)
        copy.start()
        gathers.append(copy)

    def gathered(event, dst):
        remote(dst, dst, ag_send.at[event], ag_recv.at[event], device(z, y, oc, x)).wait_recv()

    def along_z(event, zz, yy, low=0, count=ROWS, up=True):
        piece = chunk(zz, yy, c, low, count)
        gather(event, piece, piece, device(zp if up else zm, y, c, x))

    def full_z(event, yy):
        along_z(event, z, yy)
        along_z(event + 1, z, yy, up=False)

    def halves_z(event, yy):
        along_z(event + 2, zm, yy, 0, ROWS // 2)
        along_z(event + 3, zp, yy, ROWS // 2, ROWS // 2, up=False)

    def wait_full(event, yy):
        gathered(event, chunk(zm, yy, c))
        gathered(event + 1, chunk(zp, yy, c))

    def wait_halves(event, yy):
        gathered(event + 2, chunk(z2, yy, c, 0, ROWS // 2))
        gathered(event + 3, chunk(z2, yy, c, ROWS // 2, ROWS // 2))

    def along_y(j):
        piece = chunk(zs[j], yp, c)
        gather(14 + j, piece, piece, device(z, ya, c, x))

    def wait_y(j):
        gathered(14 + j, chunk(zs[j], yap, c))

    def relay(j, l):
        piece = chunk(zs[j], ys[l], c)
        gather(18 + j * 4 + l, piece, piece, device(z, y, oc, x))

    def wait_relay(j, l):
        gathered(18 + j * 4 + l, chunk(zs[j], ys[l], oc))

    gather(0, far_half, own, device(z, yp, c, x))
    gather(1, own, own, device(z, ya, c, x))
    full_z(2, y)
    relay(0, 0)

    in1[span(member, 32), :] = out1[span(member, 32), :]
    row512 = iota((512, 512), 0)
    source = (row512 & 15) * 32 + ((row512 >> 4) & 3) * 8 + (row512 >> 6)
    perm[...] = jnp.where(iota((512, 512), 1) == source, 1.0, 0.0).astype(bf16)
    for i in range(1, 16):
        other, to = member_device(i)
        landed = in1.at[span(other, 32), :]
        remote(landed, landed, r1_send.at[other], r1_recv.at[other], to).wait_recv()
    out2[...] = matmul(perm[...], in1[...]).astype(bf16)
    for i in range(1, 8):
        other, to = sub_device(i)
        launch(
            remote(
                out2.at[span(other, 64, 48), :],
                in2.at[span(sub, 48), :],
                r2_send.at[other],
                r2_recv.at[sub],
                to,
            )
        )
    in2[span(sub, 48), :] = out2[span(sub, 64, 48), :]

    gathered(0, chunk(z, yp, c))
    full_z(10, yp)
    along_y(0)
    relay(0, 1)

    for i in range(1, 8):
        other, to = sub_device(i)
        landed = in2.at[span(other, 48), :]
        remote(landed, landed, r2_send.at[other], r2_recv.at[other], to).wait_recv()
    mark = in2[:, 128:].astype(f32)
    lane = iota((SLOTS, 128), 1)
    to_place = jnp.concatenate(
        [
            jnp.where(mark == (lane + 1).astype(f32), 1.0, 0.0),
            jnp.where(mark == (lane + 129).astype(f32), 1.0, 0.0),
        ],
        axis=1,
    ).astype(bf16)
    mine = span(sub, BLOCK)
    batch[mine, :] = matmul(to_place, in2[:, :128], TN)[:BLOCK].astype(bf16)
    for i in range(1, 8):
        other, to = sub_device(i)
        launch(remote(batch.at[mine, :], batch.at[mine, :], r3_send.at[other], r3_recv.at[sub], to))

    wait_full(2, y)
    relay(1, 0)
    relay(2, 0)
    gathered(1, chunk(z, ya, c))
    relay(0, 2)

    for i in range(1, 8):
        other, to = sub_device(i)
        landed = batch.at[span(other, BLOCK), :]
        remote(landed, landed, r3_send.at[other], r3_recv.at[other], to).wait_recv()
    loads[2].wait()

    def embed(j):
        def tile(i, carry):
            rows = span(i, 128)
            v = matmul(batch[rows, :], emb[:, j * COLS : (j + 1) * COLS])
            t = jnp.tanh(v * (gelu_const + (gelu_const * cubic) * (v * v)))
            twice = v + v * t
            square = twice * twice
            total = sum(square[:, l * 128 : (l + 1) * 128] for l in range(COLS // 128))
            ssq[rows, :] = total if j == 0 else ssq[rows, :] + total
            hg[j, rows, :] = (twice * gain[j]).astype(bf16)
            return carry

        lax.fori_loop(0, TOKENS // 128, tile, 0)

    def forward(zz, kx, first=False):
        g = zz * 2 + kx

        def tile(i, carry):
            rows = span(i, 256)
            term = matmul(hg[g, rows, :], w[g])
            acc[rows, :] = term if first else acc[rows, :] + term
            return carry

        lax.fori_loop(0, TOKENS // 256, tile, 0)

    embed(0)
    embed(1)
    wait_full(10, yp)
    halves_z(10, yp)
    along_y(1)
    along_y(2)
    full_z(6, ya)
    relay(1, 1)
    relay(2, 1)
    embed(2)
    embed(3)
    wait_halves(10, yp)
    along_y(3)
    halves_z(2, y)
    relay(3, 1)
    wait_y(0)
    relay(0, 3)
    for j in range(4, 8):
        embed(j)
    for l in range(2):
        wait_relay(0, l)
    forward(z, k, first=True)
    wait_full(6, ya)
    halves_z(6, ya)
    relay(1, 2)
    relay(2, 2)
    for j in (1, 2):
        for l in range(2):
            wait_relay(j, l)
        forward(zs[j], k)
    wait_halves(2, y)
    relay(3, 0)
    for l in range(2, 4):
        wait_relay(0, l)
    forward(z, kk)
    wait_y(1)
    relay(1, 3)
    wait_y(2)
    relay(2, 3)
    for l in range(2):
        wait_relay(3, l)
    forward(z2, k)
    wait_halves(6, ya)
    relay(3, 2)
    for j in (1, 2):
        for l in range(2, 4):
            wait_relay(j, l)
        forward(zs[j], kk)
    wait_y(3)
    relay(3, 3)
    for l in range(2, 4):
        wait_relay(3, l)
    forward(z2, kk)

    loads[3].wait()
    loads[4].wait()

    def row_scale(rows):
        mean4 = jnp.sum(ssq[rows, :], axis=1, keepdims=True) * (0.25 / WIDTH)
        return lax.rsqrt(mean4 + 1e-05) * (0.5 * SCALE)

    def partial(index):
        rows = span(index, BLOCK)
        v = acc[rows, :] * row_scale(rows)
        t = jnp.tanh(v * (gelu_const + (gelu_const * cubic) * (v * v)))
        return matmul((0.5 * v * (1.0 + t)).astype(bf16), ro[...])

    for i in range(1, 8):
        other, to = sub_device(i)
        part_out[other] = partial(other).astype(bf16)
        launch(
            remote(part_out.at[other], part_in.at[sub], part_send.at[other], part_recv.at[sub], to)
        )
    part_own[...] = partial(sub)

    def slope(i, carry):
        rows = span(i, BLOCK)
        r = row_scale(rows)
        v = acc[rows, :] * r
        t = jnp.tanh(v * (gelu_const + (gelu_const * cubic) * (v * v)))
        acc[rows, :] = r * (
            0.5 * (1.0 + t)
            + (0.5 * gelu_const) * v * (1.0 - t * t) * (1.0 + (3.0 * cubic) * (v * v))
        )
        return carry

    lax.fori_loop(0, 8, slope, 0)
    total = part_own[...]
    for i in range(1, 8):
        other, to = sub_device(i)
        landed = part_in.at[other]
        remote(landed, landed, part_send.at[other], part_recv.at[other], to).wait_recv()
        total = total + part_in[other].astype(f32)
    total = total.astype(bf16)
    err_in[sub] = total
    err_own[...] = (total.astype(f32) - tgt[span(x, BLOCK), :].astype(f32)).astype(bf16)
    for i in range(4):
        other = lax.rem(x + i, 4)
        launch(
            remote(
                err_own,
                err_in.at[sub],
                err_send.at[(1 - p) * 4 + other],
                err_recv.at[sub],
                device(z, yp, c, other),
            )
        )
        if i:
            launch(
                remote(
                    err_in.at[sub],
                    err_in.at[sub],
                    err_send.at[p * 4 + other],
                    err_recv.at[sub],
                    device(z, y, c, other),
                )
            )

    def backward(index, errors):
        rows = span(index, BLOCK)
        delta[rows, :] = (matmul(errors, ro[...], NT) * acc[rows, :]).astype(bf16)

    for i in range(4):
        other = lax.rem(x + i, 4)
        index = p * 4 + other
        landed = err_in.at[index]
        if i:
            to = device(z, y, c, other)
            remote(landed, landed, err_send.at[index], err_recv.at[index], to).wait_recv()
        rows = span(other, BLOCK)
        pred_out[rows, :] = err_in[index]
        backward(index, (err_in[index].astype(f32) - tgt[rows, :].astype(f32)).astype(bf16))
    for i in range(4):
        other = lax.rem(x + i, 4)
        index = (1 - p) * 4 + other
        landed = err_in.at[index]
        to = device(z, yp, c, other)
        remote(landed, landed, err_send.at[index], err_recv.at[index], to).wait_recv()
        backward(index, err_in[index])

    for copy in gathers:
        copy.wait_send()

    def scatter(event, src, dst, to):
        launch(remote(src, dst, rs_send.at[event], rs_recv.at[event], to))

    def scattered(event, dst):
        remote(dst, dst, rs_send.at[event], rs_recv.at[event], device(z, y, oc, x)).wait_recv()

    def add(target, terms, count=ROWS):
        def tile(i, carry):
            rows = span(i, 48)
            value = target[rows, :].astype(f32)
            for term in terms:
                value = value + term[rows, :].astype(f32)
            target[rows, :] = value.astype(bf16)
            return carry

        lax.fori_loop(0, count // 48, tile, 0)

    def core_slot(zz, yy):
        start = pl.multiple_of(lax.rem(yy, 2) * ROWS, 32)
        return core_in.at[zz * 2 + lax.div(yy, 2), pl.ds(start, ROWS), :]

    def gradient(j, far):
        zz = zs[j]
        g = zz * 2 + (kk if far else k)

        def tile(i, carry):
            rows = span(i, 256)
            w[g, rows, :] = matmul(hg[g, :, rows], delta[...], TN).astype(bf16)
            return carry

        lax.fori_loop(0, 3, tile, 0)
        for l in (3, 2) if far else (0, 1):
            scatter(j * 4 + l, chunk(zz, ys[l], oc), core_slot(zz, ys[l]), device(z, y, oc, x))

    def cores(j, l):
        scattered(j * 4 + l, core_slot(zs[j], ys[l]))
        add(chunk(zs[j], ys[l], c), [core_slot(zs[j], ys[l])])

    kinds = {0: y, 1: ya, 2: yp}
    down, up = device(zm, y, c, x), device(zp, y, c, x)

    def send_halves(kind):
        yy = kinds[kind]
        event = 16 + 4 * kind
        scatter(event, chunk(z2, yy, c, 0, ROWS // 2), zhalf_in.at[kind, 0], down)
        scatter(event + 1, chunk(z2, yy, c, ROWS // 2, ROWS // 2), zhalf_in.at[kind, 1], up)

    def send_full(kind, side):
        yy = kinds[kind]
        event = 16 + 4 * kind + side
        zz = (zm, zp)[side]
        scattered(event, zhalf_in.at[kind, side])
        add(
            chunk(zz, yy, c, side * (ROWS // 2), ROWS // 2),
            [zhalf_in.at[kind, side]],
            ROWS // 2,
        )
        scatter(event + 2, chunk(zz, yy, c), zfull_in.at[kind, side], (down, up)[side])

    def wait_fulls(kind):
        for side in range(2):
            scattered(18 + 4 * kind + side, zfull_in.at[kind, side])
        return [zfull_in.at[kind, side] for side in range(2)]

    def send_y(j):
        scatter(28 + j, chunk(zs[j], yap, c), y_in.at[j], device(z, ya, c, x))

    def take_y(j):
        scattered(28 + j, y_in.at[j])
        add(chunk(zs[j], yp, c), [y_in.at[j]])

    gradient(3, True)
    gradient(3, False)
    cores(3, 3)
    send_y(3)
    cores(3, 2)
    send_halves(1)
    gradient(1, True)
    cores(3, 0)
    send_halves(0)
    gradient(2, True)
    cores(1, 3)
    send_y(1)
    gradient(1, False)
    cores(2, 3)
    send_y(2)
    cores(1, 2)
    send_full(1, 1)
    cores(2, 2)
    send_full(1, 0)
    gradient(2, False)
    cores(3, 1)
    take_y(3)
    send_halves(2)
    cores(1, 0)
    send_full(0, 1)
    gradient(0, True)
    cores(2, 0)
    send_full(0, 0)
    gradient(0, False)
    cores(0, 3)
    send_y(0)
    cores(1, 1)
    cores(2, 1)
    take_y(1)
    send_full(2, 1)
    take_y(2)
    send_full(2, 0)
    cores(0, 2)
    add(chunk(z, ya, c), wait_fulls(1))
    scatter(32, chunk(z, ya, c), y_in.at[4], device(z, ya, c, x))
    cores(0, 1)
    cores(0, 0)
    take_y(0)
    add(chunk(z, yp, c), wait_fulls(2))
    scatter(33, chunk(z, yp, c), pair_in, device(z, yp, c, x))
    terms = wait_fulls(0)
    scattered(32, y_in.at[4])
    terms = terms + [y_in.at[4]]

    def finish(i, carry):
        rows = span(i, 48)
        value = own[rows, :].astype(f32)
        for term in terms:
            value = value + term[rows, :].astype(f32)
        grad_out[rows, span(half, COLS)] = value
        return carry

    lax.fori_loop(0, ROWS // 48, finish, 0)
    scattered(33, pair_in)
    grad_out[:, span(1 - half, COLS)] = pair_in[...].astype(f32)
    for copy in sends:
        copy.wait_send()


def step(row_count, patches, group, offset, gain, embed, readout, target, master):
    vmem = pl.BlockSpec(memory_space=pltpu.VMEM)
    smem = pl.BlockSpec(memory_space=pltpu.SMEM)
    hbm = pl.BlockSpec(memory_space=pl.ANY)
    dma = pltpu.SemaphoreType.DMA
    return pl.pallas_call(
        kernel,
        out_shape=(
            jax.ShapeDtypeStruct((640, 128), bf16),
            jax.ShapeDtypeStruct((ROWS, 2 * COLS), f32),
        ),
        in_specs=[smem, vmem, vmem, vmem, vmem, hbm, hbm, hbm, hbm],
        out_specs=(vmem, vmem),
        scratch_shapes=[
            pltpu.VMEM((128, WIDTH), bf16),
            pltpu.VMEM((COLS, 128), bf16),
            pltpu.VMEM((640, 128), bf16),
            pltpu.VMEM((ROWS, COLS), f32),
            pltpu.VMEM((ROWS, COLS), f32),
            pltpu.VMEM((ROWS, COLS), bf16),
            pltpu.VMEM((8, COLS, COLS), bf16),
            pltpu.VMEM((8, TOKENS, COLS), bf16),
            pltpu.VMEM((TOKENS, COLS), f32),
            pltpu.VMEM((TOKENS, COLS), bf16),
            pltpu.VMEM((TOKENS, 128), f32),
            pltpu.VMEM((512, 512), bf16),
            pltpu.VMEM((512, 256), bf16),
            pltpu.VMEM((512, 256), bf16),
            pltpu.VMEM((512, 256), bf16),
            pltpu.VMEM((SLOTS, 256), bf16),
            pltpu.VMEM((TOKENS, 128), bf16),
            pltpu.VMEM((8, BLOCK, 128), bf16),
            pltpu.VMEM((8, BLOCK, 128), bf16),
            pltpu.VMEM((BLOCK, 128), f32),
            pltpu.VMEM((BLOCK, 128), bf16),
            pltpu.VMEM((8, BLOCK, 128), bf16),
            pltpu.VMEM((8, 2 * ROWS, COLS), bf16),
            pltpu.VMEM((3, 2, ROWS // 2, COLS), bf16),
            pltpu.VMEM((3, 2, ROWS, COLS), bf16),
            pltpu.VMEM((5, ROWS, COLS), bf16),
            pltpu.VMEM((ROWS, COLS), bf16),
            dma((5,)),
            dma((16,)),
            dma((16,)),
            dma((8,)),
            dma((8,)),
            dma((8,)),
            dma((8,)),
            dma((34,)),
            dma((34,)),
            dma((8,)),
            dma((8,)),
            dma((8,)),
            dma((8,)),
            dma((34,)),
            dma((34,)),
        ],
        compiler_params=pltpu.CompilerParams(
            collective_id=0, has_side_effects=True, vmem_limit_bytes=56 * 1024 * 1024
        ),
        name="train_step",
    )(row_count, patches, group, offset, gain, embed, readout, target, master)


def shards(
    patches,
    row_count,
    target_group,
    target_offset,
    embed,
    norm_gain,
    readout,
    target,
    master,
    moment1,
    moment2,
):
    prediction, gradient = step(
        row_count,
        patches,
        target_group.reshape(1, SLOTS),
        target_offset.reshape(1, SLOTS),
        norm_gain.astype(f32).reshape(8, 1, COLS),
        embed,
        readout,
        target,
        master,
    )
    moment1_new = beta_one * moment1 + (1.0 - beta_one) * gradient
    moment2_new = beta_two * moment2 + (1.0 - beta_two) * gradient * gradient
    first_fix = moment1_new / (1.0 - beta_one**step_count)
    second_fix = moment2_new / (1.0 - beta_two**step_count)
    master_new = master - learn_rate * (
        first_fix / (jnp.sqrt(second_fix) + adam_epsilon) + decay_rate * master
    )
    return (
        prediction.astype(f32),
        master_new,
        moment1_new,
        moment2_new,
        master_new.astype(bf16),
    )


def solution(mesh):
    placed = (
        P(("dp", "mp"), None),
        P(("dp", "mp")),
        P(("dp", "mp")),
        P(("dp", "mp")),
        P(),
        P(),
        P("mp", None),
        P("dp", None),
        P("dp", "mp"),
        P("dp", "mp"),
        P("dp", "mp"),
    )
    return jax.shard_map(
        shards,
        mesh=mesh,
        in_specs=placed,
        out_specs=(P("dp", None), P("dp", "mp"), P("dp", "mp"), P("dp", "mp"), P("dp", "mp")),
        check_vma=False,
    )
```

time: 317 us -> 144 us (0.45)
  waiting for transfers between devices: 196 us -> 0 us
  Pallas kernels: 0 us -> 133 us
  matrix products: 57 us -> 0 us
  starting transfers between devices: 16.1 us -> 0 us
  between operations: 14.6 us -> 1.33 us
  blocking collectives: 12.2 us -> 0 us
  local copies, waits for them, and re-layouts: 10.7 us -> 2.51 us
  other arithmetic: 9.67 us -> 6.35 us
    pallas_call x0 -> x1, Pallas kernels: none -> 133 us  [step(): pl.pallas_call(kernel, out_shape=(jax.ShapeDtypeStruct((640, 128), bf16),...]
    reduce_scatter x1 -> x0, waiting for transfers between devices: 122 us -> none  [shards(): lax.psum_scatter((lax.dot_general(columns, delta_rows, (((0,), (0,)), (()...]
    dot_general x4 -> x0, matrix products: 57 us -> none  [the longest x1 27.2 us: shards(): lax.dot_general(columns, delta_rows, (((0,), (0,)), ((), ())), preferred_...]
    psum x1 -> x0, waiting for transfers between devices: 40.5 us -> none  [shards(): lax.psum(jnp.dot(activation, readout, preferred_element_type=jnp.float32)...]
    all_gather x1 -> x0, waiting for transfers between devices: 19 us -> none  [shards(): lax.all_gather(weight, 'dp', axis=0, tiled=True)]
    all_to_all x2 -> x0, starting transfers between devices: 15.8 us -> none  [the longest x1 11.1 us: shards(): lax.all_to_all(slot_marks, ('dp', 'mp'), split_axis=0, concat_axis=0, til...]
    all_to_all x2 -> x0, waiting for transfers between devices: 14.5 us -> none  [the longest x1 7.87 us: shards(): lax.all_to_all(outgoing, ('dp', 'mp'), split_axis=0, concat_axis=0, tiled...]
    all_gather x1 -> x0, blocking collectives: 12.2 us -> none  [shards(): lax.all_gather(block_patches, 'mp', axis=0, tiled=True)]
  transfers between devices with their start and end apart: 5 -> 0, of which waited for: 5 -> 0; matrix products, arithmetic and copies ran while one was open for 6% -> 0% of each run, Pallas kernels for 0% -> 0%
where the time goes in v1:
time: 144 us
  Pallas kernels  133 us (92%)
  other arithmetic  6.35 us (4%)
  local copies, waits for them, and re-layouts  2.51 us (2%)
    pallas_call x1, Pallas kernels, step(): pl.pallas_call(kernel, out_shape=(jax.ShapeDtypeStruct((640, 128), bf16),...  133 us
    convert_element_type x1, other arithmetic, shards(): master_new.astype(bf16)  4.28 us

profile of v1, /device:TPU:0, one launch (start us, length us, event | category | flops | bytes accessed | tf_op | source)
XLA Modules:
  0.0 143.7 jit_solution(312534640418215904)
XLA Ops:
  0.6 1.3 reshape.25
  1.9 1.2 reshape.21.group_row
  3.2 1.2 reshape.22.offset_row
  5.1 0.0 copy-start
  5.1 0.0 copy-start.1
  5.1 133.5 %train_step.1 = (bf16[640,128]{1,0:T(8,128)(2,1)}, f32[192,1536]{1,0:T(8,128)}) custom-call(s32[1]{0:T(128)S(6)} %copy.16.row_count, bf16[384,128]{1,0:T(8,128)(2,1)} %patches.1, s32[1,384]{1,0:T(1,128)} %reshape.21.group_row, s32[1,384]{1,0:T(1,128)} %reshape.22.offset_row, f32[8,1,768]{2,1,0:T(1,128)} %bitcast.1, bf16[128,6144]{1,0:T(8,128)(2,1)} %embed_hbm.1, ...), custom_call_target="tpu_custom_call" | custom-call | tf_op jit(solution)/shard_map/train_step/pallas_call | solution.py:616
  138.6 0.0 copy-done
  138.6 0.0 copy-done.1
  138.6 0.0 copy-start.2
  138.6 4.3 %fusion.1 = (bf16[192,1536]{1,0:T(8,128)(2,1)}, f32[192,1536]{1,0:T(8,128)}, f32[192,1536]{1,0:T(8,128)}, f32[192,1536]{1,0:T(8,128)}) fusion(f32[192,1536]{1,0:T(8,128)S(1)} %copy-done, f32[192,1536]{1,0:T(8,128)} %get-tuple-element.8, f32[192,1536]{1,0:T(8,128)S(1)} %copy-done.1, f32[192,1536]{1,0:T(8,128)} %param.21), kind=kLoop, calls=%fused_computation.4 | loop fusion | flops 4718592 | bytes 8847360 | tf_op jit(solution)/shard_map/convert_element_type | solution.py:711
  142.9 0.0 copy-done.2
  142.9 0.7 convert_element_type.7
Async XLA Ops:
  5.1 133.5 %copy-start = (f32[192,1536]{1,0:T(8,128)S(1)}, f32[192,1536]{1,0:T(8,128)}, u32[]{:S(2)}) copy-start(f32[192,1536]{1,0:T(8,128)} %master_hbm.1) | copy-start | bytes 3538948
  5.1 133.5 %copy-start.1 = (f32[192,1536]{1,0:T(8,128)S(1)}, f32[192,1536]{1,0:T(8,128)}, u32[]{:S(2)}) copy-start(f32[192,1536]{1,0:T(8,128)} %param.20) | copy-start | bytes 3538948
  138.6 4.3 %copy-start.2 = (bf16[640,128]{1,0:T(8,128)(2,1)S(1)}, bf16[640,128]{1,0:T(8,128)(2,1)}, u32[]{:S(2)}) copy-start(bf16[640,128]{1,0:T(8,128)(2,1)} %get-tuple-element.7) | copy-start | bytes 491524
